TPU v7x, 32 devices: a whole 2x2x4 slice. The times are simulated.
32 devices in a mesh: groups: 2 (over y), rows: 4 (over z), cols: 4 (over x, core).
Axes of the slice: x: 2, y: 2, z: 4, core: 2. Of those that a mesh axis runs over, the one named last changes fastest.
Arguments:
- block_tiles: bfloat16 [8, 128, 256, 256], P(('groups', 'rows'), 'cols'), parts along dimension 0, may hold values from -0.0625 to 0.0625
- block_rows: int32 [8, 128], P(('groups', 'rows'), 'cols'), parts along dimension 0, may hold values from 0 to 31, as said below
- block_cols: int32 [8, 128], P(('groups', 'rows'), 'cols'), parts along dimension 0, may hold values from 0 to 31, as said below
- counts: int32 [8, 4], P(('groups', 'rows'), 'cols'), parts along dimension 0, may hold values from 16 to 32, as said below
- cell_order: int32 [8, 2048], P(('groups', 'rows')), parts along dimension 0, may hold values from 0 to 2047, each once within a row
- start_vectors: bfloat16 [16384, 128], P(('groups', 'rows')), parts along dimension 0, may hold values from 0 to 30
Outputs:
- encodings: float32 [16384, 128], P(('groups', 'rows', 'cols')), parts along dimension 0
There are 2 independent parts, one for each index of `groups`. A program takes and returns all parts, laid end to end along the dimension named above; each array names one. Nothing has to cross between parts.
Inputs may be any that keep to these rules, and one draw needn't show every extreme that they name: Every stored block has block_rows <= block_cols, its block row among the 8 blocks of its own row index. Among the stored blocks of one device, at most 1 have a block column on the cells of any one other row index; every device of a lower row index has exactly that many on the last row index. `block_cols`: drawn together with block_rows. `counts`: the devices at row index 0 hold 32 live blocks.
All inputs are finite; a program needn't handle non-finite values.
Results may differ from a plain program's by a relative error of at most 0.0072.
Values may be sent and summed in bfloat16 or wider, within the bound.
A program may use at most 64 MiB of HBM per device.

v0:
```python
import jax
import jax.numpy as jnp
from jax import lax
from jax.sharding import PartitionSpec as P

SLOTS = 1
ITERS = 2


diag_shift = 3.0
highest = lax.Precision.HIGHEST


def inverse_factor(piece, total_cells):
    local_gram = jnp.dot(piece.T, piece, precision=highest, preferred_element_type=jnp.float32)
    gram_sum = lax.psum(local_gram, ("rows", "cols"))
    lower_factor = jnp.linalg.cholesky(gram_sum / total_cells)
    identity = jnp.eye(lower_factor.shape[0], dtype=jnp.float32)
    inverse = lax.linalg.triangular_solve(lower_factor, identity, left_side=True, lower=True)
    return inverse.T


def shards(block_tiles, block_rows, block_cols, counts, cell_order, start_vectors):
    row_count = lax.axis_size("rows")
    col_count = lax.axis_size("cols")
    own_row = lax.axis_index("rows")
    own_col = lax.axis_index("cols")
    stored = block_tiles.reshape(block_tiles.shape[1], block_tiles.shape[2], block_tiles.shape[3])
    tile_count = stored.shape[0]
    block_size = stored.shape[1]
    cells_dev = cell_order.shape[1]
    blocks_dev = cells_dev // block_size
    vec_width = start_vectors.shape[1]
    quarter = cells_dev // col_count
    total_cells = cells_dev * row_count
    slot_total = row_count * SLOTS
    row_ids = block_rows.reshape(-1)
    col_ids = block_cols.reshape(-1)
    live_tiles = jnp.arange(tile_count, dtype=jnp.int32) < counts.reshape(())
    owner_row = col_ids // blocks_dev
    remote = live_tiles & (owner_row != own_row)
    near_tiles = live_tiles & (owner_row == own_row)
    local_row = row_ids - own_row * blocks_dev
    local_col = col_ids - owner_row * blocks_dev
    peer_marks = (
        (owner_row[:, None] == jnp.arange(row_count, dtype=jnp.int32)[None, :]) & remote[:, None]
    ).astype(jnp.int32)
    earlier = jnp.cumsum(peer_marks, axis=0) - peer_marks
    slot_rank = jnp.sum(earlier * peer_marks, axis=1)
    target = jnp.where(remote, owner_row * SLOTS + slot_rank, slot_total)
    slot_index = jnp.minimum(target, slot_total - 1)
    wanted = jnp.full((slot_total,), -1, jnp.int32).at[target].set(local_col, mode="drop")
    asked_ids = lax.all_to_all(
        wanted.reshape(row_count, SLOTS), "rows", split_axis=0, concat_axis=0, tiled=True
    ).reshape(-1)
    asked_live = asked_ids >= 0
    asked_safe = jnp.maximum(asked_ids, 0)
    asked_place = jnp.where(asked_live, asked_ids, blocks_dev)
    row_place = jnp.where(live_tiles, local_row, blocks_dev)
    near_place = jnp.where(near_tiles, local_col, blocks_dev)
    vectors = start_vectors[cell_order.reshape(-1)]
    result = None
    for sweep_index in range(ITERS):
        blocks = vectors.reshape(blocks_dev, block_size, vec_width)
        answer = jnp.where(asked_live[:, None, None], blocks[asked_safe], 0)
        answer = answer.reshape(row_count, SLOTS, block_size, vec_width)
        row_in = blocks[local_row]
        backward = jnp.einsum(
            "tji,tjk->tik", stored, row_in, preferred_element_type=jnp.float32
        ).astype(jnp.bfloat16)
        outgoing = (
            jnp.zeros((slot_total, block_size, vec_width), jnp.bfloat16)
            .at[target]
            .set(backward, mode="drop")
        )
        outgoing = outgoing.reshape(row_count, SLOTS, block_size, vec_width)
        fetched = lax.all_to_all(answer, "rows", split_axis=0, concat_axis=0, tiled=True)
        fetched = fetched.reshape(slot_total, block_size, vec_width)
        returned = lax.all_to_all(outgoing, "rows", split_axis=0, concat_axis=0, tiled=True)
        returned = returned.reshape(slot_total, block_size, vec_width)
        col_in = jnp.where(remote[:, None, None], fetched[slot_index], blocks[local_col])
        forward = jnp.einsum("tij,tjk->tik", stored, col_in, preferred_element_type=jnp.float32)
        partial_value = jnp.zeros((blocks_dev, block_size, vec_width), jnp.float32)
        partial_value = partial_value.at[row_place].add(forward, mode="drop")
        partial_value = partial_value.at[near_place].add(backward.astype(jnp.float32), mode="drop")
        partial_value = partial_value.at[asked_place].add(returned.astype(jnp.float32), mode="drop")
        partial_value = partial_value.reshape(cells_dev, vec_width)
        applied = lax.psum(partial_value, "cols") + diag_shift * vectors.astype(jnp.float32)
        own_part = lax.dynamic_slice_in_dim(applied, own_col * quarter, quarter, 0)
        whole_result = jnp.dot(
            applied,
            inverse_factor(own_part, total_cells),
            precision=highest,
            preferred_element_type=jnp.float32,
        )
        vectors = whole_result.astype(jnp.bfloat16)
        result = lax.dynamic_slice_in_dim(whole_result, own_col * quarter, quarter, 0)
    return result


def solution(mesh):
    in_specs = (
        P(("groups", "rows"), "cols", None, None),
        P(("groups", "rows"), "cols"),
        P(("groups", "rows"), "cols"),
        P(("groups", "rows"), "cols"),
        P(("groups", "rows"), None),
        P(("groups", "rows"), None),
    )
    out_specs = P(("groups", "rows", "cols"), None)
    return jax.shard_map(shards, mesh=mesh, in_specs=in_specs, out_specs=out_specs, check_vma=False)
```

profile of v0, /device:TPU:0, one launch (start us, length us, event | category | flops | bytes accessed | tf_op | source)
XLA Modules:
  0.0 468.4 jit_solution(12966581750035057716)
XLA Ops:
  11.6 6.3 %all-to-all-start = ((s32[4,1,1]{2,1,0:T(1,128)}), s32[4,1,1]{2,1,0:T(1,128)S(1)}, u32[]{:S(2)}, u32[]{:S(2)}) async-start(s32[4,1,1]{2,1,0:T(1,128)} %copy.52), calls=%async_computation | async-start | bytes 4096 | tf_op jit(solution)/shard_map/all_to_all | solution.py:53
  18.7 6.2 %gather_fusion = bf16[2048,128]{1,0:T(8,128)(2,1)S(1)} fusion(bf16[2048,128]{1,0:T(8,128)(2,1)S(1)} %copy-done, s32[2048]{0:T(1024)S(1)} %broadcast_clamp_fusion), kind=kCustom, calls=%fused_computation | custom fusion | bytes 1056768 | tf_op jit(solution)/shard_map/gather | solution.py:61
  24.8 2.2 gather_fusion.4
  27.0 3.7 convert_bitcast_fusion.1
  30.7 2.9 copy.58
  34.4 5.8 %scatter_fusion.2 = bf16[4,256,128]{2,1,0:T(8,128)(2,1)} fusion(bf16[4,256,128]{2,1,0:T(8,128)(2,1)} %broadcast.531.clone, s32[32]{0:T(128)S(1)} %get-tuple-element.18, bf16[32,256,128]{2,1,0:T(8,128)(2,1)} %copy.58), kind=kCustom, calls=%fused_computation.12 | custom fusion | bytes 6291584 | tf_op jit(solution)/shard_map/scatter | solution.py:74
  40.2 4.8 %all-to-all-start.2 = ((bf16[4,1,256,128]{3,2,1,0:T(8,128)(2,1)}), bf16[4,1,256,128]{3,2,1,0:T(8,128)(2,1)S(1)}, u32[]{:S(2)}, u32[]{:S(2)}) async-start(bf16[4,1,256,128]{3,2,1,0:T(8,128)(2,1)} %bitcast.24), calls=%async_computation.2 | async-start | bytes 524288 | tf_op jit(solution)/shard_map/all_to_all | solution.py:79
  45.2 1.3 gather_fusion.1
  46.6 1.8 fusion.23
  48.4 4.9 %all-to-all-done.2 = bf16[4,1,256,128]{3,2,1,0:T(8,128)(2,1)S(1)} async-done(((bf16[4,1,256,128]{3,2,1,0:T(8,128)(2,1)}), bf16[4,1,256,128]{3,2,1,0:T(8,128)(2,1)S(1)}, u32[]{:S(2)}, u32[]{:S(2)}) %all-to-all-start.2) | async-done | bytes 262176 | tf_op jit(solution)/shard_map/all_to_all | solution.py:79
  54.0 3.4 all-to-all-start.1
  57.5 3.3 copy.57
  61.8 1.8 bitcast_convert_fusion.1
  64.3 2.2 gather_fusion.2
  66.5 7.2 %fusion.8 = f32[32,256,128]{1,2,0:T(8,128)} fusion(bf16[1,32,256,256]{3,2,1,0:T(8,128)(2,1)} %param.9, bf16[32,256,128]{2,1,0:T(8,128)(2,1)} %gather_fusion.2, bf16[32,256,128]{2,1,0:T(8,128)(2,1)S(1)} %gather_fusion.3, pred[32]{0:T(512)(128)(4,1)S(1)} %compare_and_fusion), kind=kOutput, calls=%fused_computation.27 | convolution fusion | flops 537919488 | bytes 12582944 | tf_op jit(solution)/shard_map/tij,tjk->tik/dot_general | solution.py:82
  73.7 5.6 %copy.55 = f32[32,256,128]{2,1,0:T(8,128)} copy(f32[32,256,128]{1,2,0:T(8,128)} %fusion.8) | data formatting | bytes 8388608 | tf_op jit(solution)/shard_map/tij,tjk->tik/dot_general | solution.py:82
  79.4 6.4 %scatter_fusion = f32[8,256,128]{2,1,0:T(8,128)S(1)} fusion(f32[8,256,128]{2,1,0:T(8,128)S(1)} %broadcast.523.clone, s32[32]{0:T(128)S(1)} %get-tuple-element.16, f32[32,256,128]{2,1,0:T(8,128)} %copy.55), kind=kCustom, calls=%fused_computation.10 | custom fusion | flops 1048576 | bytes 12583040 | tf_op jit(solution)/shard_map/scatter-add | solution.py:84
  85.8 6.4 %scatter_fusion.1 = f32[8,256,128]{2,1,0:T(8,128)S(1)} fusion(f32[8,256,128]{2,1,0:T(8,128)S(1)} %scatter_fusion, s32[32]{0:T(128)S(1)} %get-tuple-element.6, f32[32,256,128]{2,1,0:T(8,128)} %copy.57), kind=kCustom, calls=%fused_computation.11 | custom fusion | flops 1048576 | bytes 12583040 | tf_op jit(solution)/shard_map/scatter-add | solution.py:85
  93.2 1.0 copy-done.2
  94.5 36.7 %all-reduce.5.cloned.1.call-done = f32[2048,128]{1,0:T(8,128)} async-done(((f32[2048,128]{1,0:T(8,128)}), f32[2048,128]{1,0:T(8,128)}) %all-reduce.5.cloned.1.call-update) | async-done | bytes 1048592 | tf_op jit(solution)/shard_map/psum | solution.py:88
  131.2 1.3 multiply_add_fusion.1
  132.5 1.2 fusion.26
  133.7 86.1 %all-reduce.7.cloned.1.call-done = f32[128,128]{0,1:T(8,128)} async-done(((f32[128,128]{0,1:T(8,128)}), f32[128,128]{0,1:T(8,128)}) %all-reduce.7.cloned.1.call-update) | async-done | bytes 65552 | tf_op jit(solution)/shard_map/psum | solution.py:16
  221.6 11.7 %cholesky.44 = f32[128,128]{1,0:T(8,128)S(1)} custom-call(f32[128,128]{1,0:T(8,128)S(1)} %fusion.37), custom_call_target="Cholesky" | custom-call | tf_op jit(solution)/shard_map/jit(cholesky)/cholesky | solution.py:17
  234.7 9.8 %custom-call.6 = f32[1,128,128]{1,2,0:T(8,128)S(1)} custom-call(f32[1,128,128]{2,1,0:T(8,128)S(1)} %fusion.32), custom_call_target="InvertDiagBlocksLowerTriangular" | custom-call | tf_op jit(solution)/shard_map/triangular_solve/custom-call.0 | solution.py:19
  244.8 1.0 convolution_convert_fusion
  246.4 2.1 gather_fusion.7
  248.5 2.2 gather_fusion.8
  251.5 6.2 %all-to-all-start.3 = ((bf16[4,1,256,128]{3,2,1,0:T(8,128)(2,1)}), bf16[4,1,256,128]{3,2,1,0:T(8,128)(2,1)S(1)}, u32[]{:S(2)}, u32[]{:S(2)}) async-start(bf16[4,1,256,128]{3,2,1,0:T(8,128)(2,1)} %fusion.22), calls=%async_computation.3 | async-start | bytes 524288 | tf_op jit(solution)/shard_map/all_to_all | solution.py:77
  257.7 3.7 convert_bitcast_fusion
  261.3 3.3 copy.67
  264.7 2.9 copy.68
  268.3 5.9 %scatter_fusion.6 = bf16[4,256,128]{2,1,0:T(8,128)(2,1)} fusion(bf16[4,256,128]{2,1,0:T(8,128)(2,1)} %broadcast.531, s32[32]{0:T(128)S(1)} %get-tuple-element.18, bf16[32,256,128]{2,1,0:T(8,128)(2,1)} %copy.68), kind=kCustom, calls=%fused_computation.16 | custom fusion | bytes 6291584 | tf_op jit(solution)/shard_map/scatter | solution.py:74
  274.2 4.8 %all-to-all-start.4 = ((bf16[4,1,256,128]{3,2,1,0:T(8,128)(2,1)}), bf16[4,1,256,128]{3,2,1,0:T(8,128)(2,1)}, u32[]{:S(2)}, u32[]{:S(2)}) async-start(bf16[4,1,256,128]{3,2,1,0:T(8,128)(2,1)} %bitcast.38), calls=%async_computation.4 | async-start | bytes 524288 | tf_op jit(solution)/shard_map/all_to_all | solution.py:79
  279.0 2.2 gather_fusion.6
  281.2 7.2 %fusion.11 = f32[32,256,128]{1,2,0:T(8,128)} fusion(bf16[1,32,256,256]{3,2,1,0:T(8,128)(2,1)} %param.9, bf16[32,256,128]{2,1,0:T(8,128)(2,1)} %gather_fusion.6, bf16[32,256,128]{2,1,0:T(8,128)(2,1)S(1)} %copy-done.3, pred[32]{0:T(512)(128)(4,1)S(1)} %compare_and_fusion), kind=kOutput, calls=%fused_computation.28 | convolution fusion | flops 537919488 | bytes 12582944 | tf_op jit(solution)/shard_map/tij,tjk->tik/dot_general | solution.py:82
  288.4 5.6 %copy.65 = f32[32,256,128]{2,1,0:T(8,128)} copy(f32[32,256,128]{1,2,0:T(8,128)} %fusion.11) | data formatting | bytes 8388608 | tf_op jit(solution)/shard_map/tij,tjk->tik/dot_general | solution.py:82
  294.1 6.4 %scatter_fusion.4 = f32[8,256,128]{2,1,0:T(8,128)S(1)} fusion(f32[8,256,128]{2,1,0:T(8,128)S(1)} %broadcast.523, s32[32]{0:T(128)S(1)} %get-tuple-element.16, f32[32,256,128]{2,1,0:T(8,128)} %copy.65), kind=kCustom, calls=%fused_computation.14 | custom fusion | flops 1048576 | bytes 12583040 | tf_op jit(solution)/shard_map/scatter-add | solution.py:84
  300.5 6.4 %scatter_fusion.5 = f32[8,256,128]{2,1,0:T(8,128)S(1)} fusion(f32[8,256,128]{2,1,0:T(8,128)S(1)} %scatter_fusion.4, s32[32]{0:T(128)S(1)} %get-tuple-element.6, f32[32,256,128]{2,1,0:T(8,128)} %copy.67), kind=kCustom, calls=%fused_computation.15 | custom fusion | flops 1048576 | bytes 12583040 | tf_op jit(solution)/shard_map/scatter-add | solution.py:85
  307.0 1.0 bitcast_convert_fusion
  308.9 1.0 copy-done.1
  310.0 36.7 %all-reduce.9.cloned.1.call-done = f32[2048,128]{1,0:T(8,128)} async-done(((f32[2048,128]{1,0:T(8,128)}), f32[2048,128]{1,0:T(8,128)}) %all-reduce.9.cloned.1.call-update) | async-done | bytes 1048592 | tf_op jit(solution)/shard_map/psum | solution.py:88
  346.7 1.3 multiply_add_fusion
  348.0 1.2 fusion.24
  349.3 85.9 %all-reduce.11.cloned.1.call-done = f32[128,128]{0,1:T(8,128)} async-done(((f32[128,128]{0,1:T(8,128)}), f32[128,128]{0,1:T(8,128)}) %all-reduce.11.cloned.1.call-update) | async-done | bytes 65552 | tf_op jit(solution)/shard_map/psum | solution.py:16
  437.0 11.7 %cholesky.55 = f32[128,128]{1,0:T(8,128)S(1)} custom-call(f32[128,128]{1,0:T(8,128)S(1)} %fusion.35), custom_call_target="Cholesky" | custom-call | tf_op jit(solution)/shard_map/jit(cholesky)/cholesky | solution.py:17
  450.1 9.8 %custom-call.7 = f32[1,128,128]{1,2,0:T(8,128)S(1)} custom-call(f32[1,128,128]{2,1,0:T(8,128)S(1)} %fusion.33), custom_call_target="InvertDiagBlocksLowerTriangular" | custom-call | tf_op jit(solution)/shard_map/triangular_solve/custom-call.0 | solution.py:19
  460.2 1.0 fusion.52
  (64 shorter events, 20.5 us)
Async XLA Ops:
  6.5 12.1 %copy-start = (bf16[2048,128]{1,0:T(8,128)(2,1)S(1)}, bf16[2048,128]{1,0:T(8,128)(2,1)}, u32[]{:S(2)}) copy-start(bf16[2048,128]{1,0:T(8,128)(2,1)} %param.14) | copy-start | bytes 1572868
  11.6 28.6 %all-to-all-start = ((s32[4,1,1]{2,1,0:T(1,128)}), s32[4,1,1]{2,1,0:T(1,128)S(1)}, u32[]{:S(2)}, u32[]{:S(2)}) async-start(s32[4,1,1]{2,1,0:T(1,128)} %copy.52), calls=%async_computation | async-start | bytes 4096 | tf_op jit(solution)/shard_map/all_to_all | solution.py:53
  40.2 13.1 %all-to-all-start.2 = ((bf16[4,1,256,128]{3,2,1,0:T(8,128)(2,1)}), bf16[4,1,256,128]{3,2,1,0:T(8,128)(2,1)S(1)}, u32[]{:S(2)}, u32[]{:S(2)}) async-start(bf16[4,1,256,128]{3,2,1,0:T(8,128)(2,1)} %bitcast.24), calls=%async_computation.2 | async-start | bytes 524288 | tf_op jit(solution)/shard_map/all_to_all | solution.py:79
  53.3 0.7 copy-start.5
  54.0 10.3 %all-to-all-start.1 = ((bf16[4,1,256,128]{3,2,1,0:T(8,128)(2,1)}), bf16[4,1,256,128]{3,2,1,0:T(8,128)(2,1)S(1)}, u32[]{:S(2)}, u32[]{:S(2)}) async-start(bf16[4,1,256,128]{3,2,1,0:T(8,128)(2,1)} %fusion.23), calls=%async_computation.1 | async-start | bytes 524288 | tf_op jit(solution)/shard_map/all_to_all | solution.py:77
  57.4 73.7 %all-reduce.5.cloned.1.call-start = ((), (), s32[]{:S(2)}) async-start(), calls=%async_computation.5 | async-start | bytes 2097152 | tf_op jit(solution)/shard_map/psum | solution.py:88
  85.8 6.5 %copy-start.4 = (f32[4,256,128]{2,1,0:T(8,128)S(1)}, f32[4,256,128]{2,1,0:T(8,128)}, u32[]{:S(2)}) copy-start(f32[4,256,128]{2,1,0:T(8,128)} %bitcast_convert_fusion.1) | copy-start | bytes 1572868
  93.2 1.0 copy-start.2
  94.2 125.6 %all-reduce.7.cloned.1.call-start = ((), (), s32[]{:S(2)}) async-start(), calls=%async_computation.6 | async-start | bytes 131072 | tf_op jit(solution)/shard_map/psum | solution.py:16
  251.5 22.7 %all-to-all-start.3 = ((bf16[4,1,256,128]{3,2,1,0:T(8,128)(2,1)}), bf16[4,1,256,128]{3,2,1,0:T(8,128)(2,1)S(1)}, u32[]{:S(2)}, u32[]{:S(2)}) async-start(bf16[4,1,256,128]{3,2,1,0:T(8,128)(2,1)} %fusion.22), calls=%async_computation.3 | async-start | bytes 524288 | tf_op jit(solution)/shard_map/all_to_all | solution.py:77
  274.2 32.8 %all-to-all-start.4 = ((bf16[4,1,256,128]{3,2,1,0:T(8,128)(2,1)}), bf16[4,1,256,128]{3,2,1,0:T(8,128)(2,1)}, u32[]{:S(2)}, u32[]{:S(2)}) async-start(bf16[4,1,256,128]{3,2,1,0:T(8,128)(2,1)} %bitcast.38), calls=%async_computation.4 | async-start | bytes 524288 | tf_op jit(solution)/shard_map/all_to_all | solution.py:79
  279.0 67.7 %all-reduce.9.cloned.1.call-start = ((), (), s32[]{:S(2)}) async-start(), calls=%async_computation.7 | async-start | bytes 2097152 | tf_op jit(solution)/shard_map/psum | solution.py:88
  279.0 2.2 copy-start.3
  308.9 1.0 copy-start.1
  309.9 125.3 %all-reduce.11.cloned.1.call-start = ((), (), s32[]{:S(2)}) async-start(), calls=%async_computation.8 | async-start | bytes 131072 | tf_op jit(solution)/shard_map/psum | solution.py:16
Sparse Core Ops, SparseCore 0:
  94.4 36.7 all-reduce.4
  135.0 84.7 all-reduce.6
  310.0 36.6 all-reduce.8
  350.4 84.7 all-reduce.10
where the time goes:
time: 471 us; the launch traced here: 468 us
  waiting for transfers between devices  251 us (53%)
  other arithmetic  88.7 us (19%)
  local copies, waits for them, and re-layouts  61.8 us (13%)
  matrix products  26.8 us (6%)
  starting transfers between devices  25.8 us (5%)
  between operations  14.1 us (3%)
    psum x2, waiting for transfers between devices, inverse_factor(): gram_sum = lax.psum(local_gram, ('rows', 'cols'))  172 us
    psum x2, waiting for transfers between devices, shards(): lax.psum(partial_value, 'cols') + diag_shift * vectors.astype(jnp.float32)  73.4 us
    another operation x6, other arithmetic, inverse_factor(): lower_factor = jnp.linalg.cholesky(gram_sum / total_cells)  24.8 us
    another operation x4, other arithmetic, inverse_factor(): lax.linalg.triangular_solve(lower_factor, identity, left_side=True, lower...  20.9 us
    dot_general x2, matrix products, shards(): jnp.einsum('tij,tjk->tik', stored, col_in, preferred_element_type=jnp.flo...  14.5 us
    scatter-add x2, other arithmetic, shards(): partial_value = partial_value.at[row_place].add(forward, mode='drop')  12.9 us
    scatter-add x2, other arithmetic, shards(): partial_value.at[near_place].add(backward.astype(jnp.float32), mode='drop')  12.9 us
    scatter x2, local copies, waits for them, and re-layouts, shards(): outgoing = jnp.zeros((slot_total, block_size, vec_width), jnp.bfloat16).a...  11.7 us
  transfers between devices with their start and end apart: 9, of which 6 were waited for; matrix products, arithmetic and copies ran while one was open for 16% of the time, Pallas kernels for 0%

commit v1 on v0

v1 whole, which is shorter than its diff:
```python
import functools

import jax
import jax.numpy as jnp
from jax import lax
from jax.experimental import pallas as pl
from jax.experimental.pallas import tpu as pltpu
from jax.sharding import PartitionSpec as P

ITERS = 2
MESH = pl.DeviceIdType.MESH
DIRECT = 16
diag_shift = 3.0
highest = lax.Precision.HIGHEST
f32 = jnp.float32
bf16 = jnp.bfloat16

F_TILE, F_IN, F_KEEP, G_TILE, G_IN, G_KEEP, F_LAST, G_LAST, R_TILE, R_ROW, WANT = range(11)


def route_kernel(row_count, blocks, rows_ref, cols_ref, counts_ref, tab_ref, want_ref, count, place):
    own_row = lax.axis_index("rows")
    tiles = rows_ref.shape[1]
    live_count = counts_ref[0, 0]

    def clear(i, _):
        for line in (R_TILE, WANT):
            tab_ref[line, i] = 0 if line == R_TILE else -1
        tab_ref[R_ROW, i] = -1
        return 0

    lax.fori_loop(0, row_count, clear, 0)
    for b in range(blocks + 1):
        count[0, b] = 0
        count[1, b] = 0

    def keys(t):
        col = cols_ref[0, t]
        owner = lax.div(col, blocks)
        a = rows_ref[0, t] - own_row * blocks
        b = col - owner * blocks
        live = t < live_count
        near = jnp.logical_and(live, owner == own_row)
        return a, b, owner, live, near

    def tally(t, _):
        a, b, owner, live, near = keys(t)
        ka = jnp.where(near, a, blocks)
        kb = jnp.where(near, b, blocks)
        count[0, ka] = count[0, ka] + 1
        count[1, kb] = count[1, kb] + 1

        @pl.when(jnp.logical_and(live, owner != own_row))
        def _():
            tab_ref[R_TILE, owner] = t
            tab_ref[R_ROW, owner] = a
            tab_ref[WANT, owner] = b

        return 0

    lax.fori_loop(0, tiles, tally, 0)
    for kind, last in ((0, F_LAST), (1, G_LAST)):
        total = jnp.int32(0)
        for b in range(blocks + 1):
            place[kind, b] = total
            here = count[kind, b]
            total = total + here
            if b < blocks:
                tab_ref[last, b] = jnp.where(here > 0, total, 0)
            count[kind, b] = 0

    def put(t, _):
        a, b, owner, live, near = keys(t)
        ka = jnp.where(near, a, blocks)
        kb = jnp.where(near, b, blocks)
        for kind, key, source, lines in (
            (0, ka, jnp.where(near, b, 0), (F_TILE, F_IN, F_KEEP)),
            (1, kb, jnp.where(near, a, 0), (G_TILE, G_IN, G_KEEP)),
        ):
            seen = count[kind, key]
            at = place[kind, key] + seen
            count[kind, key] = seen + 1
            tab_ref[lines[0], at] = t
            tab_ref[lines[1], at] = source
            tab_ref[lines[2], at] = jnp.minimum(seen, 1)
        return 0

    lax.fori_loop(0, tiles, put, 0)

    def wants(o, _):
        want_ref[o] = jnp.full(want_ref.shape[1:], tab_ref[WANT, o], jnp.int32)
        return 0

    lax.fori_loop(0, row_count, wants, 0)


def inverse_factor(gram):
    size = gram.shape[0]
    panels = size // 8
    lanes = lax.broadcasted_iota(jnp.int32, (8, size), 1)
    subs = lax.broadcasted_iota(jnp.int32, (8, size), 0)
    g = [gram[8 * r : 8 * r + 8, :] for r in range(panels)]
    w = [(lanes == subs + 8 * r).astype(f32) for r in range(panels)]
    done = []
    phase = 4

    def panel(_, carry):
        g, w = list(carry[0]), list(carry[1])
        n = len(g)
        col = [[jnp.broadcast_to(g[r][:, m : m + 1], (8, size)) for r in range(n)] for m in range(8)]
        pivots = jnp.ones((8, size), f32)
        for j in range(8):
            pivot = jnp.broadcast_to(col[j][0][j : j + 1, :], (8, size))
            pivots = jnp.where(subs == j, pivot, pivots)
            inv = 1.0 / pivot
            mult = [col[j][r] * inv for r in range(n)]
            mult[0] = jnp.where(subs > j, mult[0], 0.0)
            for m in range(j + 1, 8):
                row = jnp.broadcast_to(col[m][0][j : j + 1, :], (8, size))
                col[m] = [col[m][r] - mult[r] * row for r in range(n)]
            row = jnp.broadcast_to(g[0][j : j + 1, :], (8, size))
            g = [g[r] - mult[r] * row for r in range(n)]
            row = jnp.broadcast_to(w[0][j : j + 1, :], (8, size))
            w = [w[r] - mult[r] * row for r in range(n)]
        ready = w[0] * lax.rsqrt(pivots)
        g = [pltpu.roll(g[r], size - 8, 1) for r in range(1, n)] + [jnp.zeros((8, size), f32)]
        w = w[1:] + [ready]
        return tuple(g), tuple(w)

    while g:
        steps = min(phase, len(g))
        g, w = lax.fori_loop(0, steps, panel, (tuple(g), tuple(w)))
        g, w = list(g), list(w)
        keep = len(g) - steps
        done += w[keep:]
        g, w = g[:keep], w[:keep]
    return jnp.concatenate(done, axis=0)


def sweep_kernel(
    row_count, col_count, total_cells,
    tab_ref, want_ref, order_ref, start_ref, tiles_hbm, out_ref,
    tiles, near_f, near_g, vec, part, mid, app, answer, outgoing, fetched, returned, asked,
    half, cross, gram, pieces, whole, other,
    tile_sem, id_sems, ans_sems, ret_sems, half_sems, cross_sems, gat_sems, red_sems, all_sems, fly_sems,
):
    group = lax.axis_index("groups")
    row = lax.axis_index("rows")
    col = lax.axis_index("cols")
    blocks, width, block = vec.shape
    per = blocks // col_count
    tile_count = tiles.shape[0]
    low_rows = min(row_count, DIRECT // col_count)
    high_rows = row_count // low_rows
    members = low_rows * col_count
    strip = width // members
    near_col = col + 1 - 2 * lax.rem(col, 2)
    far_col = lax.rem(col + 2, 4)
    base_row = (row // low_rows) * low_rows
    own_id = (row - base_row) * col_count + col

    def every(first, last, body):
        if last - first <= 16:
            for d in range(first, last):
                body(d)
        else:
            lax.fori_loop(first, last, lambda d, c: (body(d), c)[1], 0)

    def member(e):
        q = lax.rem(own_id + e, members)
        return q, (group, base_row + q // col_count, lax.rem(q, col_count))

    def remote(src, dst, send, recv, device):
        return pltpu.make_async_remote_copy(
            src_ref=src, dst_ref=dst, send_sem=send, recv_sem=recv, device_id=device, device_id_type=MESH
        )

    load = pltpu.make_async_copy(tiles_hbm, tiles, tile_sem)
    load.start()

    barrier = pltpu.get_barrier_semaphore()

    def greet_row(d):
        pl.semaphore_signal(
            barrier, inc=1, device_id=(group, lax.rem(row + d, row_count), col), device_id_type=MESH
        )

    def greet_col(e):
        c = lax.rem(col + e, col_count)
        for r in range(low_rows):
            pl.semaphore_signal(barrier, inc=1, device_id=(group, base_row + r, c), device_id_type=MESH)

    every(1, row_count, greet_row)
    every(1, col_count, greet_col)
    pl.semaphore_wait(barrier, (row_count - 1) + (col_count - 1) * low_rows)

    def up(d):
        return (group, row + d, col)

    def down(d):
        return (group, row - d, col)

    def id_copy(d, device):
        return remote(want_ref.at[lax.rem(row + d, row_count)], asked.at[d], id_sems.at[0, d], id_sems.at[1, d], device)

    def send_ids(d):
        @pl.when(row + d < row_count)
        def _():
            id_copy(d, up(d)).start()

    every(1, row_count, send_ids)

    near_f[0] = jnp.zeros((width, block), f32)
    near_g[0] = jnp.zeros((width, block), f32)

    first = start_ref[...].astype(f32).T.astype(bf16)
    cells = first.shape[1]

    def permute(b, _):
        hit = lax.broadcasted_iota(jnp.int32, (cells, block), 0) == order_ref[b]
        vec[b] = jnp.dot(first, hit.astype(f32).astype(bf16), preferred_element_type=f32).astype(bf16)
        return 0

    lax.fori_loop(0, blocks, permute, 0)

    def finish_ids(d):
        @pl.when(row + d < row_count)
        def _():
            id_copy(d, up(d)).wait_send()

        @pl.when(row - d >= 0)
        def _():
            id_copy(d, up(d)).wait_recv()

    every(1, row_count, finish_ids)
    load.wait()

    for it in range(ITERS):

        def ans_copy(d):
            return remote(answer.at[it, d], fetched.at[it, d], ans_sems.at[it, 0, d], ans_sems.at[it, 1, d], down(d))

        def ret_copy(d):
            return remote(outgoing.at[it, d], returned.at[it, d], ret_sems.at[it, 0, d], ret_sems.at[it, 1, d], up(d))

        def send_far(d):
            @pl.when(row - d >= 0)
            def _():
                ids = asked[d][0:1, :]
                found = jnp.zeros((width, block), f32)
                for b in range(blocks):
                    found = jnp.where(ids == b, vec[b].astype(f32), found)
                answer[it, d] = found.astype(bf16)
                ans_copy(d).start()

            @pl.when(row + d < row_count)
            def _():
                peer = row + d
                a = jnp.maximum(tab_ref[R_ROW, peer], 0)
                outgoing[it, d] = jnp.dot(vec[a], tiles[tab_ref[R_TILE, peer]], preferred_element_type=f32).astype(bf16)
                ret_copy(d).start()

        every(1, row_count, send_far)

        def near(i, _):
            ahead = lax.dot_general(
                vec[tab_ref[F_IN, i]], tiles[tab_ref[F_TILE, i]], (((1,), (1,)), ((), ())), preferred_element_type=f32
            )
            near_f[i + 1] = near_f[i] * tab_ref[F_KEEP, i].astype(f32) + ahead
            back = jnp.dot(vec[tab_ref[G_IN, i]], tiles[tab_ref[G_TILE, i]], preferred_element_type=f32)
            near_g[i + 1] = near_g[i] * tab_ref[G_KEEP, i].astype(f32) + back.astype(bf16).astype(f32)
            return 0

        lax.fori_loop(0, tile_count, near, 0, unroll=2)
        for b in range(blocks):
            part[b // per, b % per] = near_f[tab_ref[F_LAST, b]] + near_g[tab_ref[G_LAST, b]]

        def take_far(d):
            @pl.when(row + d < row_count)
            def _():
                peer = row + d
                ret_copy(d).wait_send()
                ans_copy(d).wait_recv()
                ahead = lax.dot_general(
                    fetched[it, d], tiles[tab_ref[R_TILE, peer]], (((1,), (1,)), ((), ())), preferred_element_type=f32
                )
                a = tab_ref[R_ROW, peer]
                for b in range(blocks):
                    part[b // per, b % per] += ahead * (a == b).astype(f32)

            @pl.when(row - d >= 0)
            def _():
                ans_copy(d).wait_send()
                ret_copy(d).wait_recv()
                ids = asked[d][0:1, :]
                back = returned[it, d].astype(f32)
                for b in range(blocks):
                    part[b // per, b % per] += jnp.where(ids == b, back, 0.0)

        every(1, row_count, take_far)

        near_dev = (group, row, near_col)
        far_dev = (group, row, far_col)
        near_far = lax.rem(near_col + 2, 4)
        first_half = remote(part.at[near_far], half.at[it, 0], half_sems.at[it, 0, 0], half_sems.at[it, 1, 0], near_dev)
        second_half = remote(part.at[near_col], half.at[it, 1], half_sems.at[it, 0, 1], half_sems.at[it, 1, 1], near_dev)
        first_half.start()
        second_half.start()
        first_half.wait_recv()
        mid[...] = part[far_col] + half[it, 0]
        over = remote(mid, cross.at[it], cross_sems.at[it, 0], cross_sems.at[it, 1], far_dev)
        over.start()
        second_half.wait_recv()
        own = part[col] + half[it, 1]
        for k in range(per):
            app[it, col, k] = own[k] + diag_shift * vec[col * per + k].astype(f32)
        over.wait_recv()
        total = jnp.zeros((width, width), f32)
        for k in range(per):
            piece = app[it, col, k] + cross[it, k]
            app[it, col, k] = piece
            total = total + lax.dot_general(
                piece, piece, (((1,), (1,)), ((), ())), precision=highest, preferred_element_type=f32
            )
        gram[...] = total

        def red_copy(e):
            q, device = member(e)
            return remote(
                gram.at[pl.ds(pl.multiple_of(q * strip, strip), strip)],
                pieces.at[it, e], red_sems.at[it, 0, e], red_sems.at[it, 1, e], device,
            )

        mine = pl.ds(pl.multiple_of(own_id * strip, strip), strip)

        def all_copy(e):
            return remote(
                whole.at[it, mine], whole.at[it, mine], all_sems.at[it, 0, e], all_sems.at[it, 1, e], member(e)[1]
            )

        every(1, members, lambda e: red_copy(e).start())
        every(1, members, lambda e: red_copy(e).wait_recv())
        summed = gram[mine, :]
        for e in range(1, members):
            summed = summed + pieces[it, e]
        whole[it, mine] = summed
        every(1, members, lambda e: all_copy(e).start())
        every(1, members, lambda e: all_copy(e).wait_recv())
        every(1, members, lambda e: red_copy(e).wait_send())
        every(1, members, lambda e: all_copy(e).wait_send())
        gathered = whole[it]
        step = 0
        while (1 << step) < high_rows:
            span = low_rows << step
            peer = row + span - 2 * span * lax.rem(row // span, 2)
            other[it, step, 0] = gathered
            swap = remote(
                other.at[it, step, 0], other.at[it, step, 1],
                fly_sems.at[it, 0, step], fly_sems.at[it, 1, step], (group, peer, col),
            )
            swap.start()
            swap.wait()
            gathered = gathered + other[it, step, 1]
            step += 1

        last = it == ITERS - 1
        if not last:
            to_near = remote(app.at[it, col], app.at[it, col], gat_sems.at[0, 0], gat_sems.at[1, 0], near_dev)
            to_far = remote(app.at[it, col], app.at[it, col], gat_sems.at[0, 1], gat_sems.at[1, 1], far_dev)
            on = remote(app.at[it, far_col], app.at[it, far_col], gat_sems.at[0, 2], gat_sems.at[1, 2], near_dev)
            to_far.start()
            to_near.start()
        inverse = inverse_factor(gathered * (1.0 / total_cells))
        first_half.wait_send()
        second_half.wait_send()
        over.wait_send()
        if last:
            for k in range(per):
                res = jnp.dot(inverse, app[it, col, k], precision=highest, preferred_element_type=f32)
                out_ref[k * block : (k + 1) * block, :] = res.T
        else:
            to_far.wait_recv()
            on.start()
            to_near.wait_recv()
            on.wait_recv()
            to_far.wait_send()
            to_near.wait_send()
            on.wait_send()
            for b in range(blocks):
                vec[b] = jnp.dot(
                    inverse, app[it, b // per, b % per], precision=highest, preferred_element_type=f32
                ).astype(bf16)


def shards(block_tiles, block_rows, block_cols, counts, cell_order, start_vectors):
    row_count = lax.axis_size("rows")
    col_count = lax.axis_size("cols")
    stored = block_tiles.reshape(block_tiles.shape[1:])
    tile_count, block = stored.shape[0], stored.shape[1]
    cells = cell_order.shape[1]
    blocks = cells // block
    width = start_vectors.shape[1]
    per = blocks // col_count
    slots = max(row_count, tile_count, blocks)
    smem = pl.BlockSpec(memory_space=pltpu.SMEM)
    vmem = pl.BlockSpec(memory_space=pltpu.VMEM)
    table, wanted = pl.pallas_call(
        functools.partial(route_kernel, row_count, blocks),
        out_shape=(
            jax.ShapeDtypeStruct((11, slots), jnp.int32),
            jax.ShapeDtypeStruct((row_count, 8, block), jnp.int32),
        ),
        in_specs=[smem, smem, smem],
        out_specs=(smem, vmem),
        scratch_shapes=[pltpu.SMEM((2, blocks + 1), jnp.int32), pltpu.SMEM((2, blocks + 1), jnp.int32)],
    )(block_rows, block_cols, counts)
    members = min(row_count, DIRECT // col_count) * col_count
    strip = width // members
    fly = max(1, (row_count * col_count // members).bit_length() - 1)
    dma = pltpu.SemaphoreType.DMA
    return pl.pallas_call(
        functools.partial(sweep_kernel, row_count, col_count, cells * row_count),
        out_shape=jax.ShapeDtypeStruct((per * block, width), f32),
        in_specs=[smem, vmem, vmem, vmem, pl.BlockSpec(memory_space=pl.ANY)],
        out_specs=vmem,
        scratch_shapes=[
            pltpu.VMEM((tile_count, block, block), bf16),
            pltpu.VMEM((tile_count + 1, width, block), f32),
            pltpu.VMEM((tile_count + 1, width, block), f32),
            pltpu.VMEM((blocks, width, block), bf16),
            pltpu.VMEM((col_count, per, width, block), f32),
            pltpu.VMEM((per, width, block), f32),
            pltpu.VMEM((ITERS, col_count, per, width, block), f32),
            pltpu.VMEM((ITERS, row_count, width, block), bf16),
            pltpu.VMEM((ITERS, row_count, width, block), bf16),
            pltpu.VMEM((ITERS, row_count, width, block), bf16),
            pltpu.VMEM((ITERS, row_count, width, block), bf16),
            pltpu.VMEM((row_count, 8, block), jnp.int32),
            pltpu.VMEM((ITERS, 2, per, width, block), f32),
            pltpu.VMEM((ITERS, per, width, block), f32),
            pltpu.VMEM((width, width), f32),
            pltpu.VMEM((ITERS, members, strip, width), f32),
            pltpu.VMEM((ITERS, width, width), f32),
            pltpu.VMEM((ITERS, fly, 2, width, width), f32),
            dma,
            dma((2, row_count)),
            dma((ITERS, 2, row_count)),
            dma((ITERS, 2, row_count)),
            dma((ITERS, 2, 2)),
            dma((ITERS, 2)),
            dma((2, 3)),
            dma((ITERS, 2, members)),
            dma((ITERS, 2, members)),
            dma((ITERS, 2, fly)),
        ],
        compiler_params=pltpu.CompilerParams(
            collective_id=0, has_side_effects=True, vmem_limit_bytes=56 * 1024 * 1024
        ),
    )(table, wanted, cell_order.reshape(blocks, 1, block), start_vectors, stored)


def solution(mesh):
    in_specs = (
        P(("groups", "rows"), "cols", None, None),
        P(("groups", "rows"), "cols"),
        P(("groups", "rows"), "cols"),
        P(("groups", "rows"), "cols"),
        P(("groups", "rows"), None),
        P(("groups", "rows"), None),
    )
    out_specs = P(("groups", "rows", "cols"), None)
    return jax.shard_map(shards, mesh=mesh, in_specs=in_specs, out_specs=out_specs, check_vma=False)
```

time: 471 us -> 85.1 us (0.18)
  waiting for transfers between devices: 251 us -> 0 us
  other arithmetic: 88.7 us -> 0 us
  Pallas kernels: 0 us -> 82.6 us
  local copies, waits for them, and re-layouts: 61.8 us -> 1.67 us
  matrix products: 26.8 us -> 0 us
  starting transfers between devices: 25.8 us -> 0 us
  between operations: 14.1 us -> 0.67 us
    psum x4 -> x0, waiting for transfers between devices: 245 us -> none  [the longest x2 172 us: inverse_factor(): gram_sum = lax.psum(local_gram, ('rows', 'cols'))]
    pallas_call x0 -> x2, Pallas kernels: none -> 82.6 us  [the longest x1 79.7 us: shards(): pl.pallas_call(functools.partial(sweep_kernel, row_count, col_count, cell...]
    another operation x11 -> x0, other arithmetic: 45.8 us -> none  [the longest x6 24.8 us: inverse_factor(): lower_factor = jnp.linalg.cholesky(gram_sum / total_cells)]
    scatter-add x6 -> x0, other arithmetic: 27.5 us -> none  [the longest x2 12.9 us: shards(): partial_value = partial_value.at[row_place].add(forward, mode='drop')]
    dot_general x8 -> x0, matrix products: 26.2 us -> none  [the longest x2 14.5 us: shards(): jnp.einsum('tij,tjk->tik', stored, col_in, preferred_element_type=jnp.flo...]
    all_to_all x5 -> x0, starting transfers between devices: 25.5 us -> none  [the longest x2 9.59 us: shards(): lax.all_to_all(answer, 'rows', split_axis=0, concat_axis=0, tiled=True)]
    gather x9 -> x0, local copies, waits for them, and re-layouts: 19.9 us -> none  [the longest x1 6.18 us: shards(): vectors = start_vectors[cell_order.reshape(-1)]]
    convert_element_type x4 -> x0, local copies, waits for them, and re-layouts: 12.5 us -> none  [the longest x2 6.68 us: shards(): backward.astype(jnp.float32)]
  transfers between devices with their start and end apart: 9 -> 0, of which waited for: 6 -> 0; matrix products, arithmetic and copies ran while one was open for 16% -> 0% of each run, Pallas kernels for 0% -> 0%
where the time goes in v1:
time: 85.1 us; the launch traced here: 85 us
  Pallas kernels  82.6 us (97%)
  local copies, waits for them, and re-layouts  1.67 us (2%)
    pallas_call x1, Pallas kernels, shards(): pl.pallas_call(functools.partial(sweep_kernel, row_count, col_count, cell...  79.7 us
    pallas_call x1, Pallas kernels, shards(): pl.pallas_call(functools.partial(route_kernel, row_count, blocks), out_sh...  2.94 us

profile of v1, /device:TPU:0, one launch (start us, length us, event | category | flops | bytes accessed | tf_op | source)
XLA Modules:
  0.0 85.0 jit_solution(10597706127528970314)
XLA Ops:
  0.7 2.9 %shard_map.64 = (s32[11,32]{1,0:T(8,128)}, s32[4,8,256]{2,1,0:T(8,128)}) custom-call(s32[1,32]{1,0:T(1,128)} %rows_ref.1, s32[1,32]{1,0:T(1,128)} %cols_ref.1, s32[1,1]{1,0:T(1,128)S(6)} %copy.8.counts_ref), custom_call_target="tpu_custom_call" | custom-call | tf_op jit(solution)/shard_map/pallas_call | solution.py:407
  3.6 79.7 %shard_map.65 = f32[512,128]{1,0:T(8,128)} custom-call(s32[11,32]{1,0:T(8,128)} %get-tuple-element.7.tab_ref, s32[4,8,256]{2,1,0:T(8,128)} %get-tuple-element.8.want_ref, s32[8,1,256]{2,1,0:T(1,128)} %bitcast.3, bf16[2048,128]{1,0:T(8,128)(2,1)} %start_ref.1, bf16[32,256,256]{2,1,0:T(8,128)(2,1)} %bitcast.2), custom_call_target="tpu_custom_call" | custom-call | tf_op jit(solution)/shard_map/pallas_call | solution.py:421
  83.3 1.7 %copy.9 = f32[512,128]{1,0:T(8,128)} copy(f32[512,128]{1,0:T(8,128)} %shard_map.65) | data formatting | bytes 524288

commit v2 on v1

v2 whole, which is shorter than its diff:
```python
import functools

import jax
import jax.numpy as jnp
from jax import lax
from jax.experimental import pallas as pl
from jax.experimental.pallas import tpu as pltpu
from jax.sharding import PartitionSpec as P

ITERS = 2
MESH = pl.DeviceIdType.MESH
DIRECT = 4
diag_shift = 3.0
highest = lax.Precision.HIGHEST
f32 = jnp.float32
bf16 = jnp.bfloat16

F_TILE, F_IN, F_KEEP, G_TILE, G_IN, G_KEEP, F_LAST, G_LAST, R_TILE, R_ROW = range(10)


LINES = 16
LANES = 128


def route(row_count, blocks, own_row, rows_ref, cols_ref, counts_ref, lines_ref, want_ref):
    tiles = rows_ref.shape[1]
    i32 = jnp.int32
    square = (tiles, tiles)
    this = lax.broadcasted_iota(i32, square, 0)
    that = lax.broadcasted_iota(i32, square, 1)
    tile = lax.broadcasted_iota(i32, (tiles, LANES), 0)
    lane = lax.broadcasted_iota(i32, (tiles, LANES), 1)

    def count(flags, axis):
        return jnp.sum(jnp.where(flags, 1, 0), axis=axis, keepdims=True)

    def upright(line):
        return jnp.sum(jnp.where(this == that, jnp.broadcast_to(line, square), 0), axis=1, keepdims=True)

    def pick(flags, value):
        return jnp.sum(jnp.where(flags, value, 0), axis=0, keepdims=True)

    cols = cols_ref[...]
    owner = jnp.zeros(cols.shape, i32)
    for o in range(1, row_count):
        owner = owner + jnp.where(cols >= o * blocks, 1, 0)
    a = rows_ref[...] - own_row * blocks
    b = cols - owner * blocks
    live = jnp.where(lax.broadcasted_iota(i32, cols.shape, 1) < counts_ref[0, 0], 1, 0)
    local = jnp.where(owner == own_row, 1, 0)
    near = live * local
    for key, source, lines in ((a, b, (F_TILE, F_IN, F_KEEP, F_LAST)), (b, a, (G_TILE, G_IN, G_KEEP, G_LAST))):
        key = jnp.where(near > 0, key, blocks)
        own_key = upright(key)
        other = jnp.broadcast_to(key, square)
        equal = jnp.logical_and(other == own_key, that < this)
        seen = count(equal, 1)
        rank = count(other < own_key, 1) + seen
        here = rank == lane
        lines_ref[lines[0] : lines[0] + 1, :] = pick(here, tile)
        lines_ref[lines[1] : lines[1] + 1, :] = pick(here, upright(source * near))
        lines_ref[lines[2] : lines[2] + 1, :] = pick(here, jnp.minimum(seen, 1))
        lines_ref[lines[3] : lines[3] + 1, :] = jnp.where(count(own_key == lane, 0) > 0, count(own_key <= lane, 0), 0)
    far = jnp.logical_and(upright(owner) == lane, upright(live * (1 - local)) > 0)
    lines_ref[R_TILE : R_TILE + 1, :] = pick(far, tile)
    lines_ref[R_ROW : R_ROW + 1, :] = pick(far, upright(a) + 1) - 1
    want = pick(far, upright(b) + 1) - 1
    for o in range(row_count):
        want_ref[o] = jnp.broadcast_to(want[:, o : o + 1], want_ref.shape[1:])


def inverse_factor(gram):
    size = gram.shape[0]
    panels = size // 8
    lanes = lax.broadcasted_iota(jnp.int32, (8, size), 1)
    subs = lax.broadcasted_iota(jnp.int32, (8, size), 0)
    g = [gram[8 * r : 8 * r + 8, :] for r in range(panels)]
    w = [(lanes == subs + 8 * r).astype(f32) for r in range(panels)]
    done = []
    phase = 4

    def spread(x, j):
        return jnp.broadcast_to(x[j : j + 1, :], (8, size))

    def panel(i, carry):
        g, w = list(carry[0]), list(carry[1])
        n = len(g)
        p, q = jnp.where(lanes < size - 8 * i, g[0], 0.0), w[0]
        col = [jnp.broadcast_to(p[:, m : m + 1], (8, size)) for m in range(8)]
        pivots = jnp.ones((8, size), f32)
        for j in range(0, 8, 2):
            k = j + 1
            one, low, up, two = spread(col[j], j), spread(col[j], k), spread(col[k], j), spread(col[k], k)
            det = one * two - low * up
            inv = 1.0 / one
            inv_det = 1.0 / det
            step = low * inv
            pivots = jnp.where(subs == j, one, jnp.where(subs == k, det * inv, pivots))
            first = jnp.where(subs > j, col[j] * inv, 0.0)
            second = jnp.where(subs > k, (col[k] - first * up) * (one * inv_det), 0.0)

            def clear(x):
                top = spread(x, j)
                return x - first * top - second * (spread(x, k) - step * top)

            for m in range(j + 2, 8):
                col[m] = clear(col[m])
            p, q = clear(p), clear(q)
        factors = jnp.transpose(p / pivots)
        p_rows = [spread(p, j) for j in range(8)]
        q_rows = [spread(q, j) for j in range(8)]
        for r in range(1, n):
            for j in range(8):
                mult = jnp.broadcast_to(factors[8 * r : 8 * r + 8, j : j + 1], (8, size))
                g[r] = g[r] - mult * p_rows[j]
                w[r] = w[r] - mult * q_rows[j]
        g = [pltpu.roll(g[r], size - 8, 1) for r in range(1, n)] + [jnp.zeros((8, size), f32)]
        w = w[1:] + [q * lax.rsqrt(pivots)]
        return tuple(g), tuple(w)

    at = 0
    while g:
        steps = min(phase, len(g))
        g, w = lax.fori_loop(at, at + steps, panel, (tuple(g), tuple(w)))
        g, w = list(g), list(w)
        at += steps
        keep = len(g) - steps
        done += w[keep:]
        g, w = g[:keep], w[:keep]
    return jnp.concatenate(done, axis=0)


def sweep_kernel(
    row_count, col_count, total_cells,
    rows_ref, cols_ref, counts_ref, order_ref, start_ref, tiles_hbm, out_ref, inverse_ref,
    lines_ref, tab_ref, want_ref,
    tiles, near_f, near_g, vec, part, mid, app, answer, outgoing, fetched, returned, asked,
    half, cross, part16, mid16, half16, cross16, gram, pieces, strips, whole, other,
    tile_sem, tab_sem, id_sems, ans_sems, ret_sems, half_sems, cross_sems, gat_sems, red_sems, row_sems, all_sems, fly_sems,
):
    group = lax.axis_index("groups")
    row = lax.axis_index("rows")
    col = lax.axis_index("cols")
    blocks, width, block = vec.shape
    per = blocks // col_count
    tile_count = tiles.shape[0]
    low_rows = min(row_count, DIRECT)
    high_rows = row_count // low_rows
    strip = width // col_count
    near_col = col + 1 - 2 * lax.rem(col, 2)
    far_col = lax.rem(col + 2, 4)
    base_row = (row // low_rows) * low_rows
    low_row = row - base_row

    def every(first, last, body):
        if last - first <= 16:
            for d in range(first, last):
                body(d)
        else:
            lax.fori_loop(first, last, lambda d, c: (body(d), c)[1], 0)

    def remote(src, dst, send, recv, device):
        return pltpu.make_async_remote_copy(
            src_ref=src, dst_ref=dst, send_sem=send, recv_sem=recv, device_id=device, device_id_type=MESH
        )

    load = pltpu.make_async_copy(tiles_hbm, tiles, tile_sem)
    load.start()

    barrier = pltpu.get_barrier_semaphore()

    def greet_row(d):
        pl.semaphore_signal(
            barrier, inc=1, device_id=(group, lax.rem(row + d, row_count), col), device_id_type=MESH
        )

    def greet_col(e):
        pl.semaphore_signal(
            barrier, inc=1, device_id=(group, row, lax.rem(col + e, col_count)), device_id_type=MESH
        )

    every(1, row_count, greet_row)
    every(1, col_count, greet_col)
    route(row_count, blocks, row, rows_ref, cols_ref, counts_ref, lines_ref, want_ref)
    table = pltpu.make_async_copy(lines_ref, tab_ref, tab_sem)
    table.start()
    pl.semaphore_wait(barrier, (row_count - 1) + (col_count - 1))

    def up(d):
        return (group, row + d, col)

    def down(d):
        return (group, row - d, col)

    def id_copy(d, device):
        return remote(want_ref.at[lax.rem(row + d, row_count)], asked.at[d], id_sems.at[0, d], id_sems.at[1, d], device)

    def send_ids(d):
        @pl.when(row + d < row_count)
        def _():
            id_copy(d, up(d)).start()

    every(1, row_count, send_ids)

    near_f[0] = jnp.zeros((width, block), f32)
    near_g[0] = jnp.zeros((width, block), f32)

    first = start_ref[...].astype(f32).T.astype(bf16)
    cells = first.shape[1]

    def permute(b, _):
        hit = lax.broadcasted_iota(jnp.int32, (cells, block), 0) == order_ref[b]
        vec[b] = jnp.dot(first, hit.astype(f32).astype(bf16), preferred_element_type=f32).astype(bf16)
        return 0

    lax.fori_loop(0, blocks, permute, 0)

    def finish_ids(d):
        @pl.when(row + d < row_count)
        def _():
            id_copy(d, up(d)).wait_send()

        @pl.when(row - d >= 0)
        def _():
            id_copy(d, up(d)).wait_recv()

    every(1, row_count, finish_ids)
    table.wait()
    load.wait()

    for it in range(ITERS):

        def ans_copy(d):
            return remote(answer.at[it, d], fetched.at[it, d], ans_sems.at[it, 0, d], ans_sems.at[it, 1, d], down(d))

        def ret_copy(d):
            return remote(outgoing.at[it, d], returned.at[it, d], ret_sems.at[it, 0, d], ret_sems.at[it, 1, d], up(d))

        def send_far(d):
            @pl.when(row - d >= 0)
            def _():
                ids = asked[d][0:1, :]
                found = jnp.zeros((width, block), f32)
                for b in range(blocks):
                    found = jnp.where(ids == b, vec[b].astype(f32), found)
                answer[it, d] = found.astype(bf16)
                ans_copy(d).start()

            @pl.when(row + d < row_count)
            def _():
                peer = row + d
                a = jnp.maximum(tab_ref[R_ROW, peer], 0)
                outgoing[it, d] = jnp.dot(vec[a], tiles[tab_ref[R_TILE, peer]], preferred_element_type=f32).astype(bf16)
                ret_copy(d).start()

        every(1, row_count, send_far)

        def near(i, _):
            ahead = lax.dot_general(
                vec[tab_ref[F_IN, i]], tiles[tab_ref[F_TILE, i]], (((1,), (1,)), ((), ())), preferred_element_type=f32
            )
            near_f[i + 1] = near_f[i] * tab_ref[F_KEEP, i].astype(f32) + ahead
            back = jnp.dot(vec[tab_ref[G_IN, i]], tiles[tab_ref[G_TILE, i]], preferred_element_type=f32)
            near_g[i + 1] = near_g[i] * tab_ref[G_KEEP, i].astype(f32) + back.astype(bf16).astype(f32)
            return 0

        lax.fori_loop(0, tile_count, near, 0, unroll=2)
        for b in range(blocks):
            part[b // per, b % per] = near_f[tab_ref[F_LAST, b]] + near_g[tab_ref[G_LAST, b]]

        def take_far(d):
            @pl.when(row + d < row_count)
            def _():
                peer = row + d
                ret_copy(d).wait_send()
                ans_copy(d).wait_recv()
                ahead = lax.dot_general(
                    fetched[it, d], tiles[tab_ref[R_TILE, peer]], (((1,), (1,)), ((), ())), preferred_element_type=f32
                )
                a = tab_ref[R_ROW, peer]
                for b in range(blocks):
                    part[b // per, b % per] += ahead * (a == b).astype(f32)

            @pl.when(row - d >= 0)
            def _():
                ans_copy(d).wait_send()
                ret_copy(d).wait_recv()
                ids = asked[d][0:1, :]
                back = returned[it, d].astype(f32)
                for b in range(blocks):
                    part[b // per, b % per] += jnp.where(ids == b, back, 0.0)

        every(1, row_count, take_far)

        last = it == ITERS - 1
        near_dev = (group, row, near_col)
        far_dev = (group, row, far_col)
        near_far = lax.rem(near_col + 2, 4)
        if last:
            part16[near_far] = part[near_far].astype(bf16)
            part16[near_col] = part[near_col].astype(bf16)
        out, arrived, sent, crossed = (part16, half16, mid16, cross16) if last else (part, half, mid, cross)
        first_half = remote(out.at[near_far], arrived.at[0], half_sems.at[it, 0, 0], half_sems.at[it, 1, 0], near_dev)
        second_half = remote(out.at[near_col], arrived.at[1], half_sems.at[it, 0, 1], half_sems.at[it, 1, 1], near_dev)
        first_half.start()
        second_half.start()
        first_half.wait_recv()
        sent[...] = (part[far_col] + arrived[0].astype(f32)).astype(sent.dtype)
        over = remote(sent, crossed, cross_sems.at[it, 0], cross_sems.at[it, 1], far_dev)
        over.start()
        second_half.wait_recv()
        own = part[col] + arrived[1].astype(f32)
        for k in range(per):
            part[col, k] = own[k] + diag_shift * vec[col * per + k].astype(f32)
        over.wait_recv()
        for k in range(per):
            piece = part[col, k] + crossed[k].astype(f32)
            if last:
                out_ref[k] = piece
            else:
                app[col, k] = piece

        def gat_copy(kind, k, quarter, device):
            place = app.at[quarter, k]
            return remote(place, place, gat_sems.at[0, kind, k], gat_sems.at[1, kind, k], device)

        to_far = [gat_copy(0, k, col, far_dev) for k in range(per)]
        to_near = [gat_copy(1, k, col, near_dev) for k in range(per)]
        onward = [gat_copy(2, k, far_col, near_dev) for k in range(per)]
        total = jnp.zeros((width, width), f32)
        for k in range(per):
            piece = out_ref[k] if last else app[col, k]
            total = total + lax.dot_general(
                piece, piece, (((1,), (1,)), ((), ())), precision=highest, preferred_element_type=f32
            )
        gram[...] = total

        def peer_col(e):
            return (group, row, lax.rem(col + e, col_count))

        def red_copy(e):
            q = lax.rem(col + e, col_count)
            return remote(
                gram.at[pl.ds(pl.multiple_of(q * strip, strip), strip)],
                pieces.at[it, e], red_sems.at[it, 0, e], red_sems.at[it, 1, e], peer_col(e),
            )

        def row_copy(d):
            place = strips.at[it, low_row]
            device = (group, base_row + lax.rem(low_row + d, low_rows), col)
            return remote(place, place, row_sems.at[it, 0, d], row_sems.at[it, 1, d], device)

        mine = pl.ds(pl.multiple_of(col * strip, strip), strip)

        def all_copy(e):
            place = whole.at[it, mine]
            return remote(place, place, all_sems.at[it, 0, e], all_sems.at[it, 1, e], peer_col(e))

        every(1, col_count, lambda e: red_copy(e).start())
        every(1, col_count, lambda e: red_copy(e).wait_recv())
        summed = gram[mine, :]
        for e in range(1, col_count):
            summed = summed + pieces[it, e]
        strips[it, low_row] = summed
        every(1, low_rows, lambda d: row_copy(d).start())
        every(1, low_rows, lambda d: row_copy(d).wait_recv())
        summed = strips[it, 0]
        for d in range(1, low_rows):
            summed = summed + strips[it, d]
        step = 0
        while (1 << step) < high_rows:
            span = low_rows << step
            peer = row + span - 2 * span * lax.rem(row // span, 2)
            other[it, step, 0] = summed
            swap = remote(
                other.at[it, step, 0], other.at[it, step, 1],
                fly_sems.at[it, 0, step], fly_sems.at[it, 1, step], (group, peer, col),
            )
            swap.start()
            swap.wait()
            summed = summed + other[it, step, 1]
            step += 1
        whole[it, mine] = summed
        every(1, col_count, lambda e: all_copy(e).start())
        every(1, col_count, lambda e: all_copy(e).wait_recv())
        if not last:
            for k in range(per):
                to_far[k].start()
                to_near[k].start()
        if not last:
            for k in range(per):
                pass
        inverse = inverse_factor(whole[it] * (1.0 / total_cells))
        every(1, col_count, lambda e: red_copy(e).wait_send())
        every(1, low_rows, lambda d: row_copy(d).wait_send())
        every(1, col_count, lambda e: all_copy(e).wait_send())
        first_half.wait_send()
        second_half.wait_send()
        over.wait_send()
        if last:
            inverse_ref[...] = inverse
        else:
            for k in range(per):
                to_far[k].wait_recv()
                onward[k].start()
            for k in range(per):
                to_near[k].wait_recv()
                onward[k].wait_recv()
                to_far[k].wait_send()
                to_near[k].wait_send()
                onward[k].wait_send()
            for b in range(blocks):
                vec[b] = jnp.dot(
                    inverse, app[b // per, b % per], precision=highest, preferred_element_type=f32
                ).astype(bf16)


def shards(block_tiles, block_rows, block_cols, counts, cell_order, start_vectors):
    row_count = lax.axis_size("rows")
    col_count = lax.axis_size("cols")
    stored = block_tiles.reshape(block_tiles.shape[1:])
    tile_count, block = stored.shape[0], stored.shape[1]
    cells = cell_order.shape[1]
    blocks = cells // block
    width = start_vectors.shape[1]
    per = blocks // col_count
    smem = pl.BlockSpec(memory_space=pltpu.SMEM)
    vmem = pl.BlockSpec(memory_space=pltpu.VMEM)
    low_rows = min(row_count, DIRECT)
    strip = width // col_count
    fly = max(1, (row_count // low_rows).bit_length() - 1)
    dma = pltpu.SemaphoreType.DMA
    applied, inverse = pl.pallas_call(
        functools.partial(sweep_kernel, row_count, col_count, cells * row_count),
        out_shape=(jax.ShapeDtypeStruct((per, width, block), f32), jax.ShapeDtypeStruct((width, width), f32)),
        in_specs=[vmem, vmem, smem, vmem, vmem, pl.BlockSpec(memory_space=pl.ANY)],
        out_specs=(vmem, vmem),
        scratch_shapes=[
            pltpu.VMEM((LINES, LANES), jnp.int32),
            pltpu.SMEM((LINES, LANES), jnp.int32),
            pltpu.VMEM((row_count, 8, block), jnp.int32),
            pltpu.VMEM((tile_count, block, block), bf16),
            pltpu.VMEM((tile_count + 1, width, block), f32),
            pltpu.VMEM((tile_count + 1, width, block), f32),
            pltpu.VMEM((blocks, width, block), bf16),
            pltpu.VMEM((col_count, per, width, block), f32),
            pltpu.VMEM((per, width, block), f32),
            pltpu.VMEM((col_count, per, width, block), f32),
            pltpu.VMEM((ITERS, row_count, width, block), bf16),
            pltpu.VMEM((ITERS, row_count, width, block), bf16),
            pltpu.VMEM((ITERS, row_count, width, block), bf16),
            pltpu.VMEM((ITERS, row_count, width, block), bf16),
            pltpu.VMEM((row_count, 8, block), jnp.int32),
            pltpu.VMEM((2, per, width, block), f32),
            pltpu.VMEM((per, width, block), f32),
            pltpu.VMEM((col_count, per, width, block), bf16),
            pltpu.VMEM((per, width, block), bf16),
            pltpu.VMEM((2, per, width, block), bf16),
            pltpu.VMEM((per, width, block), bf16),
            pltpu.VMEM((width, width), f32),
            pltpu.VMEM((ITERS, col_count, strip, width), f32),
            pltpu.VMEM((ITERS, low_rows, strip, width), f32),
            pltpu.VMEM((ITERS, width, width), f32),
            pltpu.VMEM((ITERS, fly, 2, strip, width), f32),
            dma,
            dma,
            dma((2, row_count)),
            dma((ITERS, 2, row_count)),
            dma((ITERS, 2, row_count)),
            dma((ITERS, 2, 2)),
            dma((ITERS, 2)),
            dma((2, 3, per)),
            dma((ITERS, 2, col_count)),
            dma((ITERS, 2, low_rows)),
            dma((ITERS, 2, col_count)),
            dma((ITERS, 2, fly)),
        ],
        compiler_params=pltpu.CompilerParams(
            collective_id=0, has_side_effects=True, vmem_limit_bytes=56 * 1024 * 1024
        ),
    )(block_rows, block_cols, counts, cell_order.reshape(blocks, 1, block), start_vectors, stored)
    result = jnp.einsum("kwb,vw->kbv", applied, inverse, precision=highest, preferred_element_type=f32)
    return result.reshape(per * block, width)


def solution(mesh):
    in_specs = (
        P(("groups", "rows"), "cols", None, None),
        P(("groups", "rows"), "cols"),
        P(("groups", "rows"), "cols"),
        P(("groups", "rows"), "cols"),
        P(("groups", "rows"), None),
        P(("groups", "rows"), None),
    )
    out_specs = P(("groups", "rows", "cols"), None)
    return jax.shard_map(shards, mesh=mesh, in_specs=in_specs, out_specs=out_specs, check_vma=False)
```

time: 85.1 us -> 81 us (0.952)
  Pallas kernels: 82.6 us -> 78 us
  matrix products: 0 us -> 2.25 us
  local copies, waits for them, and re-layouts: 1.67 us -> 0 us
    pallas_call x1 -> x0, Pallas kernels: 2.94 us -> none  [shards(): pl.pallas_call(functools.partial(route_kernel, row_count, blocks), out_sh...]
    dot_general x0 -> x1, matrix products: none -> 2.25 us  [shards(): jnp.einsum('kwb,vw->kbv', applied, inverse, precision=highest, preferred_...]
    pallas_call x1, Pallas kernels: 79.7 us -> 78 us  [shards(): pl.pallas_call(functools.partial(sweep_kernel, row_count, col_count, cell...]
    unnamed x1 -> x0, local copies, waits for them, and re-layouts: 1.67 us -> none
where the time goes in v2:
time: 81 us; the launch traced here: 80.9 us
  Pallas kernels  78 us (96%)
  matrix products  2.25 us (3%)
    pallas_call x1, Pallas kernels, shards(): pl.pallas_call(functools.partial(sweep_kernel, row_count, col_count, cell...  78 us
    dot_general x1, matrix products, shards(): jnp.einsum('kwb,vw->kbv', applied, inverse, precision=highest, preferred_...  2.25 us

profile of v2, /device:TPU:0, one launch (start us, length us, event | category | flops | bytes accessed | tf_op | source)
XLA Modules:
  0.0 80.9 jit_solution(4708761849399480399)
XLA Ops:
  0.7 78.0 %shard_map.64 = (f32[2,128,256]{2,1,0:T(8,128)}, f32[128,128]{1,0:T(8,128)}) custom-call(s32[1,32]{1,0:T(1,128)} %rows_ref.1, s32[1,32]{1,0:T(1,128)} %cols_ref.1, s32[1,1]{1,0:T(1,128)S(6)} %copy.9.counts_ref, s32[8,1,256]{2,1,0:T(1,128)} %bitcast.8, bf16[2048,128]{1,0:T(8,128)(2,1)} %start_ref.1, bf16[32,256,256]{2,1,0:T(8,128)(2,1)} %bitcast.7), custom_call_target="tpu_custom_call" | custom-call | tf_op jit(solution)/shard_map/pallas_call | solution.py:433
  78.6 2.2 %fusion = f32[2,256,128]{2,1,0:T(8,128)} fusion(f32[2,128,256]{2,1,0:T(8,128)} %get-tuple-element.7, f32[128,128]{1,0:T(8,128)} %get-tuple-element.8), kind=kOutput, calls=%fused_computation | convolution fusion | flops 100663296 | bytes 589824 | tf_op jit(solution)/shard_map/kwb,vw->kbv/dot_general | solution.py:482

commit v3 on v2

--- a/solution.py
+++ b/solution.py
@@ -69,7 +69,7 @@
         want_ref[o] = jnp.broadcast_to(want[:, o : o + 1], want_ref.shape[1:])
 
 
-def inverse_factor(gram):
+def inverse_factor(gram, aside):
     size = gram.shape[0]
     panels = size // 8
     lanes = lax.broadcasted_iota(jnp.int32, (8, size), 1)
@@ -124,6 +124,8 @@
         g, w = lax.fori_loop(at, at + steps, panel, (tuple(g), tuple(w)))
         g, w = list(g), list(w)
         at += steps
+        if len(g) == 2 * phase:
+            aside()
         keep = len(g) - steps
         done += w[keep:]
         g, w = g[:keep], w[:keep]
@@ -134,9 +136,9 @@
     row_count, col_count, total_cells,
     rows_ref, cols_ref, counts_ref, order_ref, start_ref, tiles_hbm, out_ref, inverse_ref,
     lines_ref, tab_ref, want_ref,
-    tiles, near_f, near_g, vec, part, mid, app, answer, outgoing, fetched, returned, asked,
-    half, cross, part16, mid16, half16, cross16, gram, pieces, strips, whole, other,
-    tile_sem, tab_sem, id_sems, ans_sems, ret_sems, half_sems, cross_sems, gat_sems, red_sems, row_sems, all_sems, fly_sems,
+    tiles, near_f, near_g, vec, part, app, answer, outgoing, fetched, returned, asked,
+    half, part16, mid16, half16, cross16, gram, pieces, strips, whole, other, common, share, shared,
+    tile_sem, tab_sem, share_sems, id_sems, ans_sems, ret_sems, half_sems, cross_sems, gat_sems, red_sems, row_sems, all_sems, fly_sems,
 ):
     group = lax.axis_index("groups")
     row = lax.axis_index("rows")
@@ -184,6 +186,22 @@
     route(row_count, blocks, row, rows_ref, cols_ref, counts_ref, lines_ref, want_ref)
     table = pltpu.make_async_copy(lines_ref, tab_ref, tab_sem)
     table.start()
+    first = start_ref[...].astype(f32).T.astype(bf16)
+    cells = first.shape[1]
+
+    def permute(b, _):
+        hit = lax.broadcasted_iota(jnp.int32, (cells, block), 0) == order_ref[b]
+        vec[b] = jnp.dot(first, hit.astype(f32).astype(bf16), preferred_element_type=f32).astype(bf16)
+        return 0
+
+    lax.fori_loop(0, blocks, permute, 0)
+    mean = vec[0].astype(f32)
+    for b in range(1, blocks):
+        mean = mean + vec[b].astype(f32)
+    mean = jnp.sum(mean, axis=1, keepdims=True) * (1.0 / cells)
+    scale = lax.rsqrt(jnp.maximum(jnp.sum(mean * mean, axis=0, keepdims=True), 1e-30))
+    common[...] = jnp.broadcast_to(mean * scale, common.shape)
+
     pl.semaphore_wait(barrier, (row_count - 1) + (col_count - 1))
 
     def up(d):
@@ -205,16 +223,6 @@
     near_f[0] = jnp.zeros((width, block), f32)
     near_g[0] = jnp.zeros((width, block), f32)
 
-    first = start_ref[...].astype(f32).T.astype(bf16)
-    cells = first.shape[1]
-
-    def permute(b, _):
-        hit = lax.broadcasted_iota(jnp.int32, (cells, block), 0) == order_ref[b]
-        vec[b] = jnp.dot(first, hit.astype(f32).astype(bf16), preferred_element_type=f32).astype(bf16)
-        return 0
-
-    lax.fori_loop(0, blocks, permute, 0)
-
     def finish_ids(d):
         @pl.when(row + d < row_count)
         def _():
@@ -224,7 +232,6 @@
         def _():
             id_copy(d, up(d)).wait_recv()
 
-    every(1, row_count, finish_ids)
     table.wait()
     load.wait()
 
@@ -236,7 +243,7 @@
         def ret_copy(d):
             return remote(outgoing.at[it, d], returned.at[it, d], ret_sems.at[it, 0, d], ret_sems.at[it, 1, d], up(d))
 
-        def send_far(d):
+        def send_down(d):
             @pl.when(row - d >= 0)
             def _():
                 ids = asked[d][0:1, :]
@@ -246,6 +253,7 @@
                 answer[it, d] = found.astype(bf16)
                 ans_copy(d).start()
 
+        def send_up(d):
             @pl.when(row + d < row_count)
             def _():
                 peer = row + d
@@ -253,7 +261,9 @@
                 outgoing[it, d] = jnp.dot(vec[a], tiles[tab_ref[R_TILE, peer]], preferred_element_type=f32).astype(bf16)
                 ret_copy(d).start()
 
-        every(1, row_count, send_far)
+        every(1, row_count, send_up)
+        if it > 0:
+            every(1, row_count, send_down)
 
         def near(i, _):
             ahead = lax.dot_general(
@@ -264,7 +274,12 @@
             near_g[i + 1] = near_g[i] * tab_ref[G_KEEP, i].astype(f32) + back.astype(bf16).astype(f32)
             return 0
 
-        lax.fori_loop(0, tile_count, near, 0, unroll=2)
+        early = tile_count // 4 if it == 0 else 0
+        if it == 0:
+            lax.fori_loop(0, early, near, 0, unroll=2)
+            every(1, row_count, finish_ids)
+            every(1, row_count, send_down)
+        lax.fori_loop(early, tile_count, near, 0, unroll=2)
         for b in range(blocks):
             part[b // per, b % per] = near_f[tab_ref[F_LAST, b]] + near_g[tab_ref[G_LAST, b]]
 
@@ -299,29 +314,40 @@
         if last:
             part16[near_far] = part[near_far].astype(bf16)
             part16[near_col] = part[near_col].astype(bf16)
-        out, arrived, sent, crossed = (part16, half16, mid16, cross16) if last else (part, half, mid, cross)
+        out, arrived = (part16, half16) if last else (part, half)
+        sent, crossed = mid16.at[it], cross16.at[it]
+        shares = remote(share, shared, share_sems.at[0], share_sems.at[1], far_dev)
         first_half = remote(out.at[near_far], arrived.at[0], half_sems.at[it, 0, 0], half_sems.at[it, 1, 0], near_dev)
         second_half = remote(out.at[near_col], arrived.at[1], half_sems.at[it, 0, 1], half_sems.at[it, 1, 1], near_dev)
         first_half.start()
         second_half.start()
         first_half.wait_recv()
-        sent[...] = (part[far_col] + arrived[0].astype(f32)).astype(sent.dtype)
+        for k in range(per):
+            value = part[far_col, k] + arrived[0, k].astype(f32)
+            if not last:
+                along = jnp.sum(common[...] * value, axis=0, keepdims=True)
+                share[k] = jnp.broadcast_to(along, share.shape[1:])
+                value = value - common[...] * along
+            sent[k] = value.astype(bf16)
+        if not last:
+            shares.start()
         over = remote(sent, crossed, cross_sems.at[it, 0], cross_sems.at[it, 1], far_dev)
         over.start()
         second_half.wait_recv()
         own = part[col] + arrived[1].astype(f32)
         for k in range(per):
             part[col, k] = own[k] + diag_shift * vec[col * per + k].astype(f32)
+        if not last:
+            shares.wait_recv()
         over.wait_recv()
         for k in range(per):
             piece = part[col, k] + crossed[k].astype(f32)
-            if last:
-                out_ref[k] = piece
-            else:
-                app[col, k] = piece
+            if not last:
+                piece = piece + common[...] * shared[k, 0:1, :]
+            app[it, col, k] = piece
 
         def gat_copy(kind, k, quarter, device):
-            place = app.at[quarter, k]
+            place = app.at[it, quarter, k]
             return remote(place, place, gat_sems.at[0, kind, k], gat_sems.at[1, kind, k], device)
 
         to_far = [gat_copy(0, k, col, far_dev) for k in range(per)]
@@ -329,7 +355,7 @@
         onward = [gat_copy(2, k, far_col, near_dev) for k in range(per)]
         total = jnp.zeros((width, width), f32)
         for k in range(per):
-            piece = out_ref[k] if last else app[col, k]
+            piece = app[it, col, k]
             total = total + lax.dot_general(
                 piece, piece, (((1,), (1,)), ((), ())), precision=highest, preferred_element_type=f32
             )
@@ -357,7 +383,14 @@
             return remote(place, place, all_sems.at[it, 0, e], all_sems.at[it, 1, e], peer_col(e))
 
         every(1, col_count, lambda e: red_copy(e).start())
+        if last:
+            for k in range(per):
+                out_ref[k * block : (k + 1) * block, :] = app[it, col, k].T
         every(1, col_count, lambda e: red_copy(e).wait_recv())
+        if not last:
+            to_far[0].start()
+            for k in range(per):
+                to_near[k].start()
         summed = gram[mine, :]
         for e in range(1, col_count):
             summed = summed + pieces[it, e]
@@ -384,25 +417,29 @@
         every(1, col_count, lambda e: all_copy(e).start())
         every(1, col_count, lambda e: all_copy(e).wait_recv())
         if not last:
-            for k in range(per):
+            to_far[0].wait_recv()
+            onward[0].start()
+            for k in range(1, per):
                 to_far[k].start()
-                to_near[k].start()
-        if not last:
-            for k in range(per):
-                pass
-        inverse = inverse_factor(whole[it] * (1.0 / total_cells))
+
+        def pass_on():
+            if not last:
+                for k in range(1, per):
+                    to_far[k].wait_recv()
+                    onward[k].start()
+
+        inverse = inverse_factor(whole[it] * (1.0 / total_cells), pass_on)
         every(1, col_count, lambda e: red_copy(e).wait_send())
         every(1, low_rows, lambda d: row_copy(d).wait_send())
         every(1, col_count, lambda e: all_copy(e).wait_send())
         first_half.wait_send()
         second_half.wait_send()
         over.wait_send()
+        if not last:
+            shares.wait_send()
         if last:
             inverse_ref[...] = inverse
         else:
-            for k in range(per):
-                to_far[k].wait_recv()
-                onward[k].start()
             for k in range(per):
                 to_near[k].wait_recv()
                 onward[k].wait_recv()
@@ -411,7 +448,7 @@
                 onward[k].wait_send()
             for b in range(blocks):
                 vec[b] = jnp.dot(
-                    inverse, app[b // per, b % per], precision=highest, preferred_element_type=f32
+                    inverse, app[it, b // per, b % per], precision=highest, preferred_element_type=f32
                 ).astype(bf16)
 
 
@@ -432,7 +469,7 @@
     dma = pltpu.SemaphoreType.DMA
     applied, inverse = pl.pallas_call(
         functools.partial(sweep_kernel, row_count, col_count, cells * row_count),
-        out_shape=(jax.ShapeDtypeStruct((per, width, block), f32), jax.ShapeDtypeStruct((width, width), f32)),
+        out_shape=(jax.ShapeDtypeStruct((per * block, width), f32), jax.ShapeDtypeStruct((width, width), f32)),
         in_specs=[vmem, vmem, smem, vmem, vmem, pl.BlockSpec(memory_space=pl.ANY)],
         out_specs=(vmem, vmem),
         scratch_shapes=[
@@ -444,26 +481,28 @@
             pltpu.VMEM((tile_count + 1, width, block), f32),
             pltpu.VMEM((blocks, width, block), bf16),
             pltpu.VMEM((col_count, per, width, block), f32),
-            pltpu.VMEM((per, width, block), f32),
-            pltpu.VMEM((col_count, per, width, block), f32),
+            pltpu.VMEM((ITERS, col_count, per, width, block), f32),
             pltpu.VMEM((ITERS, row_count, width, block), bf16),
             pltpu.VMEM((ITERS, row_count, width, block), bf16),
             pltpu.VMEM((ITERS, row_count, width, block), bf16),
             pltpu.VMEM((ITERS, row_count, width, block), bf16),
             pltpu.VMEM((row_count, 8, block), jnp.int32),
             pltpu.VMEM((2, per, width, block), f32),
-            pltpu.VMEM((per, width, block), f32),
             pltpu.VMEM((col_count, per, width, block), bf16),
-            pltpu.VMEM((per, width, block), bf16),
+            pltpu.VMEM((ITERS, per, width, block), bf16),
             pltpu.VMEM((2, per, width, block), bf16),
-            pltpu.VMEM((per, width, block), bf16),
+            pltpu.VMEM((ITERS, per, width, block), bf16),
             pltpu.VMEM((width, width), f32),
             pltpu.VMEM((ITERS, col_count, strip, width), f32),
             pltpu.VMEM((ITERS, low_rows, strip, width), f32),
             pltpu.VMEM((ITERS, width, width), f32),
             pltpu.VMEM((ITERS, fly, 2, strip, width), f32),
+            pltpu.VMEM((width, block), f32),
+            pltpu.VMEM((per, 8, block), f32),
+            pltpu.VMEM((per, 8, block), f32),
             dma,
             dma,
+            dma((2,)),
             dma((2, row_count)),
             dma((ITERS, 2, row_count)),
             dma((ITERS, 2, row_count)),
@@ -479,8 +518,9 @@
             collective_id=0, has_side_effects=True, vmem_limit_bytes=56 * 1024 * 1024
         ),
     )(block_rows, block_cols, counts, cell_order.reshape(blocks, 1, block), start_vectors, stored)
-    result = jnp.einsum("kwb,vw->kbv", applied, inverse, precision=highest, preferred_element_type=f32)
-    return result.reshape(per * block, width)
+    return lax.dot_general(
+        applied, inverse, (((1,), (1,)), ((), ())), precision=highest, preferred_element_type=f32
+    )
 
 
 def solution(mesh):

time: 81 us -> 76.4 us (0.943)
  Pallas kernels: 78 us -> 73.6 us
    pallas_call x1, Pallas kernels: 78 us -> 73.6 us  [shards(): pl.pallas_call(functools.partial(sweep_kernel, row_count, col_count, cell...]
where the time goes in v3:
time: 76.4 us; the launch traced here: 76.3 us
  Pallas kernels  73.6 us (96%)
  matrix products  2.03 us (3%)
    pallas_call x1, Pallas kernels, shards(): pl.pallas_call(functools.partial(sweep_kernel, row_count, col_count, cell...  73.6 us
    dot_general x1, matrix products, shards(): lax.dot_general(applied, inverse, (((1,), (1,)), ((), ())), precision=hig...  2.03 us

profile of v3, /device:TPU:0, one launch (start us, length us, event | category | flops | bytes accessed | tf_op | source)
XLA Modules:
  0.0 76.3 jit_solution(15295450841307402213)
XLA Ops:
  0.7 73.6 %shard_map.64 = (f32[512,128]{1,0:T(8,128)}, f32[128,128]{1,0:T(8,128)}) custom-call(s32[1,32]{1,0:T(1,128)} %rows_ref.1, s32[1,32]{1,0:T(1,128)} %cols_ref.1, s32[1,1]{1,0:T(1,128)S(6)} %copy.7.counts_ref, s32[8,1,256]{2,1,0:T(1,128)} %bitcast.5, bf16[2048,128]{1,0:T(8,128)(2,1)} %start_ref.1, bf16[32,256,256]{2,1,0:T(8,128)(2,1)} %bitcast.4), custom_call_target="tpu_custom_call" | custom-call | tf_op jit(solution)/shard_map/pallas_call | solution.py:470
  74.2 2.0 %fusion = f32[512,128]{1,0:T(8,128)} fusion(f32[512,128]{1,0:T(8,128)} %get-tuple-element.7, f32[128,128]{1,0:T(8,128)} %get-tuple-element.8), kind=kOutput, calls=%fused_computation | convolution fusion | flops 100663296 | bytes 589824 | tf_op jit(solution)/shard_map/dot_general | solution.py:521

commit v4 on v3

--- a/solution.py
+++ b/solution.py
@@ -156,7 +156,7 @@
 
     def every(first, last, body):
         if last - first <= 16:
-            for d in range(first, last):
+            for d in reversed(range(first, last)):
                 body(d)
         else:
             lax.fori_loop(first, last, lambda d, c: (body(d), c)[1], 0)
@@ -317,30 +317,39 @@
         out, arrived = (part16, half16) if last else (part, half)
         sent, crossed = mid16.at[it], cross16.at[it]
         shares = remote(share, shared, share_sems.at[0], share_sems.at[1], far_dev)
-        first_half = remote(out.at[near_far], arrived.at[0], half_sems.at[it, 0, 0], half_sems.at[it, 1, 0], near_dev)
-        second_half = remote(out.at[near_col], arrived.at[1], half_sems.at[it, 0, 1], half_sems.at[it, 1, 1], near_dev)
-        first_half.start()
+        first_half = [
+            remote(out.at[near_far, k], arrived.at[0, k], half_sems.at[it, 0, k], half_sems.at[it, 1, k], near_dev)
+            for k in range(per)
+        ]
+        second_half = remote(
+            out.at[near_col], arrived.at[1], half_sems.at[it, 0, per], half_sems.at[it, 1, per], near_dev
+        )
+        over = [
+            remote(sent.at[k], crossed.at[k], cross_sems.at[it, 0, k], cross_sems.at[it, 1, k], far_dev)
+            for k in range(per)
+        ]
+        for k in range(per):
+            first_half[k].start()
         second_half.start()
-        first_half.wait_recv()
         for k in range(per):
+            first_half[k].wait_recv()
             value = part[far_col, k] + arrived[0, k].astype(f32)
             if not last:
                 along = jnp.sum(common[...] * value, axis=0, keepdims=True)
                 share[k] = jnp.broadcast_to(along, share.shape[1:])
                 value = value - common[...] * along
             sent[k] = value.astype(bf16)
+            over[k].start()
         if not last:
             shares.start()
-        over = remote(sent, crossed, cross_sems.at[it, 0], cross_sems.at[it, 1], far_dev)
-        over.start()
         second_half.wait_recv()
         own = part[col] + arrived[1].astype(f32)
         for k in range(per):
             part[col, k] = own[k] + diag_shift * vec[col * per + k].astype(f32)
         if not last:
             shares.wait_recv()
-        over.wait_recv()
         for k in range(per):
+            over[k].wait_recv()
             piece = part[col, k] + crossed[k].astype(f32)
             if not last:
                 piece = piece + common[...] * shared[k, 0:1, :]
@@ -432,9 +441,10 @@
         every(1, col_count, lambda e: red_copy(e).wait_send())
         every(1, low_rows, lambda d: row_copy(d).wait_send())
         every(1, col_count, lambda e: all_copy(e).wait_send())
-        first_half.wait_send()
         second_half.wait_send()
-        over.wait_send()
+        for k in range(per):
+            first_half[k].wait_send()
+            over[k].wait_send()
         if not last:
             shares.wait_send()
         if last:
@@ -506,8 +516,8 @@
             dma((2, row_count)),
             dma((ITERS, 2, row_count)),
             dma((ITERS, 2, row_count)),
-            dma((ITERS, 2, 2)),
-            dma((ITERS, 2)),
+            dma((ITERS, 2, per + 1)),
+            dma((ITERS, 2, per)),
             dma((2, 3, per)),
             dma((ITERS, 2, col_count)),
             dma((ITERS, 2, low_rows)),

time: 76.4 us -> 76.2 us (level)
  no operation moved by 1% of the time
where the time goes in v4:
time: 76.2 us; the launch traced here: 76 us
  Pallas kernels  73.3 us (96%)
  matrix products  2.03 us (3%)
    pallas_call x1, Pallas kernels, shards(): pl.pallas_call(functools.partial(sweep_kernel, row_count, col_count, cell...  73.3 us
    dot_general x1, matrix products, shards(): lax.dot_general(applied, inverse, (((1,), (1,)), ((), ())), precision=hig...  2.03 us

profile of v4, /device:TPU:0, one launch (start us, length us, event | category | flops | bytes accessed | tf_op | source)
XLA Modules:
  0.0 76.0 jit_solution(3600555612298859112)
XLA Ops:
  0.7 73.3 %shard_map.64 = (f32[512,128]{1,0:T(8,128)}, f32[128,128]{1,0:T(8,128)}) custom-call(s32[1,32]{1,0:T(1,128)} %rows_ref.1, s32[1,32]{1,0:T(1,128)} %cols_ref.1, s32[1,1]{1,0:T(1,128)S(6)} %copy.7.counts_ref, s32[8,1,256]{2,1,0:T(1,128)} %bitcast.5, bf16[2048,128]{1,0:T(8,128)(2,1)} %start_ref.1, bf16[32,256,256]{2,1,0:T(8,128)(2,1)} %bitcast.4), custom_call_target="tpu_custom_call" | custom-call | tf_op jit(solution)/shard_map/pallas_call | solution.py:480
  74.0 2.0 %fusion = f32[512,128]{1,0:T(8,128)} fusion(f32[512,128]{1,0:T(8,128)} %get-tuple-element.7, f32[128,128]{1,0:T(8,128)} %get-tuple-element.8), kind=kOutput, calls=%fused_computation | convolution fusion | flops 100663296 | bytes 589824 | tf_op jit(solution)/shard_map/dot_general | solution.py:531
